TPU v7x, 32 devices: a whole 2x2x4 slice. The times are simulated.
32 devices in a mesh: groups: 2 (over y), seq: 4 (over z), chan: 4 (over x, core).
Axes of the slice: x: 2, y: 2, z: 4, core: 2. Of those that a mesh axis runs over, the one named last changes fastest.
Arguments:
- query: bfloat16 [16384, 1024], P(('groups', 'seq'), 'chan'), parts along dimension 0, may hold values from -6 to 6
- keyed: bfloat16 [16384, 1024], P(('groups', 'seq'), 'chan'), parts along dimension 0, may hold values from -6 to 6
- values: bfloat16 [16384, 1024], P(('groups', 'seq'), 'chan'), parts along dimension 0, may hold values from -6 to 6
- cotangent: bfloat16 [16384, 1024], P(('groups', 'seq'), 'chan'), parts along dimension 0, may hold values from -6 to 6
- segment_ids: int32 [16384], P(('groups', 'seq')), parts along dimension 0, may hold values from 0 to 7, never falling along the last dimension, each value on 1 to 2048 neighbouring positions
- positions: bfloat16 [16384, 64], P(('groups', 'seq')), parts along dimension 0, may hold values from -6 to 6
- filter_weight: bfloat16 [64, 1024], P('seq', 'chan'), may hold values from -0.75 to 0.75
- skip_gain: float32 [1024], P('chan'), may hold values from 0.5 to 1.5
- first_factor: bfloat16 [256, 256], replicated, may hold values from -0.375 to 0.375
- second_factor: bfloat16 [8, 8], replicated, may hold values from -2 to 2
- self_coef: bfloat16 [2, 4, 2048], P(None, 'seq'), may hold values from -4 to 4
- cross_coef: bfloat16 [2, 4, 2048], P(None, 'seq'), may hold values from -4 to 4
Outputs:
- mixed: bfloat16 [16384, 1024], P(('groups', 'seq'), 'chan'), parts along dimension 0
- grad_query: bfloat16 [16384, 1024], P(('groups', 'seq'), 'chan'), parts along dimension 0
- grad_keyed: bfloat16 [16384, 1024], P(('groups', 'seq'), 'chan'), parts along dimension 0
- grad_values: bfloat16 [16384, 1024], P(('groups', 'seq'), 'chan'), parts along dimension 0
- grad_filter: float32 [128, 1024], P(('groups', 'seq'), 'chan'), parts along dimension 0
There are 2 independent parts, one for each index of `groups`. A program takes and returns all parts, laid end to end along the dimension named above; an argument that names none is the same for every part. Nothing has to cross between parts.
Inputs may be any that keep to these rules, and one draw needn't show every extreme that they name: `segment_ids`: document numbers never fall along the sequence; each document holds 1 to 2048 positions and one holds exactly 2048.
All inputs are finite; a program needn't handle non-finite values.
Results may differ from a plain program's by a relative error of at most 0.014.
Values may be sent and summed in bfloat16 or wider, within the bound.
A program may use at most 64 MiB of HBM per device.

v0:
```python
import functools
import math

import jax
import jax.numpy as jnp
from jax import lax
from jax.experimental import pallas as pl
from jax.experimental.pallas import tpu as pltpu
from jax.sharding import PartitionSpec as P

BLK = 256
LANES = 128
F32 = jnp.float32
BF16 = jnp.bfloat16


def kernel(
    count, sections, scale,
    query, keyed, values, cotangent, keep_in, ends, pos, weight, gain, first, second, coefs,
    mixed, grad_query, grad_keyed, grad_values, grad_filter,
    first_t, keep_t, u_all, gt_all, half, fwd_send, fwd_recv, back_send, back_recv,
    pos_send, pos_recv, weight_send, weight_recv, ends_recv, coef_recv, coef_t,
    weight_lo, weight_hi, filt, dw_keep, dfilt, part_send, part_recv,
    field_send_sem, field_recv_sem, small_send_sem, small_recv_sem, ends_sem,
):
    rows, width = query.shape
    groups = rows // BLK
    quarter = rows // count
    packed = quarter // 2
    feats = pos.shape[1]
    share = weight.shape[0]
    chunks = width // LANES
    me = lax.axis_index("seq")
    others = [(k, lax.rem(me + k, count)) for k in range(1, count)]
    sources = [(k, lax.rem(me + count - k, count)) for k in range(1, count)]

    barrier = pltpu.get_barrier_semaphore()
    for _, other in others:
        pl.semaphore_signal(barrier, inc=1, device_id={"seq": other}, device_id_type=pl.DeviceIdType.MESH)

    def remote(src, dst, send, recv, other):
        return pltpu.make_async_remote_copy(
            src_ref=src, dst_ref=dst, send_sem=send, recv_sem=recv,
            device_id={"seq": other}, device_id_type=pl.DeviceIdType.MESH,
        )

    for p in range(count):
        block = pos[p * quarter:(p + 1) * quarter, :]
        pos_send[p] = jnp.concatenate([block[:packed], block[packed:]], axis=1)
    weight_send[...] = weight[...].astype(F32)
    first_t[...] = first[...].astype(F32).T.astype(BF16)

    pl.semaphore_wait(barrier, count - 1)

    def small(kind, k, other):
        send, recv = small_send_sem.at[kind, k], small_recv_sem.at[kind, k]
        if kind == 0:
            return remote(pos_send.at[other], pos_recv.at[me], send, recv, other)
        if kind == 1:
            return remote(weight_send, weight_recv.at[me], send, recv, other)
        if kind == 2:
            return remote(coefs.at[other], coef_recv.at[me], send, recv, other)
        return remote(part_send.at[other], part_recv.at[me], send, recv, other)

    ring = remote(ends.at[1], ends_recv, ends_sem.at[0], ends_sem.at[1], lax.rem(me + 1, count))
    ring.start()
    for kind in (2, 1, 0):
        for k, other in others:
            small(kind, k, other).start()
    pos_recv[me] = pos_send[me]
    weight_recv[me] = weight_send[...]
    coef_recv[me] = coefs[me]

    def forward_copy(unit, k, other):
        return remote(
            fwd_send.at[unit, other], fwd_recv.at[unit, me],
            field_send_sem.at[0, unit, k], field_recv_sem.at[0, unit, k], other,
        )

    def back_copy(unit, k, other):
        return remote(
            back_send.at[unit, other], back_recv.at[unit, me],
            field_send_sem.at[1, unit, k], field_recv_sem.at[1, unit, k], other,
        )

    def lanes(chunk):
        return slice(chunk * LANES, (chunk + 1) * LANES)

    step = min(16, quarter)
    mat = [[second[j, i] for i in range(groups)] for j in range(groups)]

    def forward(unit, chunk, source):
        for j in range(groups):
            x = source[j * BLK:(j + 1) * BLK, lanes(chunk)]
            half[j] = jnp.dot(first_t[...], x, preferred_element_type=F32).astype(BF16)

        @pl.loop(0, BLK // step)
        def _(r):
            at = pl.multiple_of(r * step, step)
            xs = [half[j, pl.ds(at, step), :].astype(F32) for j in range(groups)]
            for i in range(groups):
                y = mat[0][i] * xs[0]
                for j in range(1, groups):
                    y = y + mat[j][i] * xs[j]
                place = i * BLK + at
                fwd_send[unit, place // quarter, pl.ds(pl.multiple_of(lax.rem(place, quarter), step), step), :] = y.astype(BF16)

        for k, other in others:
            forward_copy(unit, k, other).start()
        fwd_recv[unit, me] = fwd_send[unit, me]

    for j in range(groups):
        at = slice(j * BLK, (j + 1) * BLK)
        gt_all[at, :] = (cotangent[at, :].astype(F32) * query[at, :].astype(F32)).astype(BF16)
    for chunk in range(chunks):
        forward(chunk, chunk, gt_all)

    ring.wait_recv()
    same = jnp.where((ends[0] == ends_recv[...]) & (me > 0), 1.0, 0.0)
    spot = (lax.broadcasted_iota(jnp.int32, keep_in.shape, 0) == 0) & (lax.broadcasted_iota(jnp.int32, keep_in.shape, 1) == 0)
    keep_t[...] = jnp.where(spot, same, keep_in[...]).T
    for j in range(groups):
        at = slice(j * BLK, (j + 1) * BLK)
        u_all[at, :] = (keyed[at, :].astype(F32) * values[at, :].astype(F32) * keep_t[:, j:j + 1]).astype(BF16)
    for chunk in range(chunks):
        forward(chunks + chunk, chunk, u_all)

    for kind in (2, 1, 0):
        for k, source in sources:
            small(kind, k, source).wait_recv()
    weight_lo[...] = jnp.zeros_like(weight_lo)
    weight_hi[...] = jnp.zeros_like(weight_hi)
    for p in range(count):
        weight_lo[p * share:(p + 1) * share, :] = weight_recv[p]
        weight_hi[feats + p * share:feats + (p + 1) * share, :] = weight_recv[p]
    low, high = weight_lo[...].astype(BF16), weight_hi[...].astype(BF16)
    for p in range(count):
        filt[p, :packed, :] = jnp.dot(pos_recv[p], low, preferred_element_type=F32)
        filt[p, packed:, :] = jnp.dot(pos_recv[p], high, preferred_element_type=F32)
        coef_t[p] = coef_recv[p].T

    def rounded(x):
        return x.astype(BF16).astype(F32)

    def middle(unit, chunk, gated):
        for k, source in sources:
            forward_copy(unit, k, source).wait_recv()

        @pl.loop(0, quarter // step)
        def _(r):
            at = pl.ds(pl.multiple_of(r * step, step), step)
            xs = [fwd_recv[unit, p, at, :].astype(F32) for p in range(count)]
            cols = [coef_t[p, at, :] for p in range(count)]

            def own(k, p):
                return cols[p][:, k:k + 1]

            def cross(k, p):
                return cols[p][:, sections + k:sections + k + 1]

            for k in range(sections):
                xs = [rounded(own(k, p) * xs[p] + cross(k, p) * xs[p ^ (1 << k)]) for p in range(count)]
            for p in range(count):
                if gated:
                    dw_keep[chunk, p, at, :] = xs[p].astype(BF16)
                else:
                    dfilt[p, at, :] = (dw_keep[chunk, p, at, :].astype(F32) * xs[p]).astype(BF16)
            xs = [rounded(xs[p] * filt[p, at, lanes(chunk)]) for p in range(count)]
            for k in reversed(range(sections)):
                xs = [
                    rounded(own(k, p) * xs[p] + cross(k, p ^ (1 << k)) * xs[p ^ (1 << k)])
                    for p in range(count)
                ]
            for p in range(count):
                back_send[unit, p, at, :] = xs[p].astype(BF16)

        for k, other in others:
            back_copy(unit, k, other).start()
        back_recv[unit, me] = back_send[unit, me]
        if not gated:
            over = (((0,), (0,)), ((), ()))
            lo = jnp.zeros((2 * feats, LANES), F32)
            hi = jnp.zeros((2 * feats, LANES), F32)
            for p in range(count):
                lo = lo + lax.dot_general(pos_recv[p], dfilt[p, :packed, :], over, preferred_element_type=F32)
                hi = hi + lax.dot_general(pos_recv[p], dfilt[p, packed:, :], over, preferred_element_type=F32)
            total = (lo[:feats] + hi[feats:]) * scale
            for p in range(count):
                part_send[p, :, lanes(chunk)] = total[p * share:(p + 1) * share]

    for chunk in range(chunks):
        middle(chunk, chunk, True)
    for chunk in range(chunks):
        middle(chunks + chunk, chunk, False)
    for k, other in others:
        small(3, k, other).start()
    part_recv[me] = part_send[me]

    def final(unit, chunk, gated):
        for k, source in sources:
            back_copy(unit, k, source).wait_recv()

        @pl.loop(0, BLK // step)
        def _(r):
            at = pl.multiple_of(r * step, step)
            xs = []
            for i in range(groups):
                place = i * BLK + at
                xs.append(back_recv[unit, place // quarter, pl.ds(pl.multiple_of(lax.rem(place, quarter), step), step), :].astype(F32))
            for j in range(groups):
                y = mat[j][0] * xs[0]
                for i in range(1, groups):
                    y = y + mat[j][i] * xs[i]
                half[j, pl.ds(at, step), :] = y.astype(BF16)

        skip = gain[0:1, lanes(chunk)]
        cut = lanes(chunk)
        for j in range(groups):
            at = slice(j * BLK, (j + 1) * BLK)
            y = rounded(jnp.dot(first[...], half[j], preferred_element_type=F32))
            if gated:
                du = (y + skip * gt_all[at, cut].astype(F32)) * keep_t[:, j:j + 1]
                grad_keyed[at, cut] = (du * values[at, cut].astype(F32)).astype(BF16)
                grad_values[at, cut] = (du * keyed[at, cut].astype(F32)).astype(BF16)
            else:
                total = y + skip * u_all[at, cut].astype(F32)
                mixed[at, cut] = (query[at, cut].astype(F32) * total).astype(BF16)
                grad_query[at, cut] = (cotangent[at, cut].astype(F32) * total).astype(BF16)

    for chunk in range(chunks):
        final(chunk, chunk, True)
    for chunk in range(chunks):
        final(chunks + chunk, chunk, False)

    for k, source in sources:
        small(3, k, source).wait_recv()
    total = part_recv[0]
    for p in range(1, count):
        total = total + part_recv[p]
    grad_filter[...] = total

    ring.wait_send()
    for k, other in others:
        for kind in range(4):
            small(kind, k, other).wait_send()
        for unit in range(2 * chunks):
            forward_copy(unit, k, other).wait_send()
            back_copy(unit, k, other).wait_send()


def on_device(
    query, keyed, values, cotangent, segment_ids, positions, filter_weight, skip_gain,
    first_factor, second_factor, self_coef, cross_coef,
):
    count = lax.axis_size("seq")
    sections = self_coef.shape[0]
    rows, width = query.shape
    groups = rows // BLK
    quarter = rows // count
    feats = positions.shape[1]
    share = filter_weight.shape[0]
    chunks = width // LANES
    units = 2 * chunks
    kinds = -(-2 * sections // 8) * 8
    before = jnp.concatenate([segment_ids[:1], segment_ids[:-1]])
    keep = (segment_ids == before).astype(F32).reshape(groups, BLK)
    ends = jnp.broadcast_to(jnp.stack([segment_ids[0], segment_ids[-1]])[:, None, None], (2, groups, BLK))
    coefs = jnp.concatenate([self_coef[:, 0], cross_coef[:, 0]]).astype(F32)
    coefs = jnp.pad(coefs, ((0, kinds - 2 * sections), (0, 0)))
    coefs = coefs.reshape(kinds, count, quarter).transpose(1, 0, 2)
    scale = 1.0 / math.sqrt(rows * count)
    vmem = pl.BlockSpec(memory_space=pltpu.VMEM)
    smem = pl.BlockSpec(memory_space=pltpu.SMEM)
    field = jax.ShapeDtypeStruct((rows, width), BF16)
    return pl.pallas_call(
        functools.partial(kernel, count, sections, scale),
        out_shape=(field, field, field, field, jax.ShapeDtypeStruct((share, width), F32)),
        in_specs=[vmem] * 10 + [smem, vmem],
        out_specs=(vmem,) * 5,
        scratch_shapes=[
            pltpu.VMEM((BLK, BLK), BF16),
            pltpu.VMEM((BLK, groups), F32),
            pltpu.VMEM((rows, width), BF16),
            pltpu.VMEM((rows, width), BF16),
            pltpu.VMEM((groups, BLK, LANES), BF16),
            pltpu.VMEM((units, count, quarter, LANES), BF16),
            pltpu.VMEM((units, count, quarter, LANES), BF16),
            pltpu.VMEM((units, count, quarter, LANES), BF16),
            pltpu.VMEM((units, count, quarter, LANES), BF16),
            pltpu.VMEM((count, quarter // 2, 2 * feats), BF16),
            pltpu.VMEM((count, quarter // 2, 2 * feats), BF16),
            pltpu.VMEM((share, width), F32),
            pltpu.VMEM((count, share, width), F32),
            pltpu.VMEM((groups, BLK), jnp.int32),
            pltpu.VMEM((count, kinds, quarter), F32),
            pltpu.VMEM((count, quarter, kinds), F32),
            pltpu.VMEM((2 * feats, width), F32),
            pltpu.VMEM((2 * feats, width), F32),
            pltpu.VMEM((count, quarter, width), F32),
            pltpu.VMEM((chunks, count, quarter, LANES), BF16),
            pltpu.VMEM((count, quarter, LANES), BF16),
            pltpu.VMEM((count, share, width), F32),
            pltpu.VMEM((count, share, width), F32),
            pltpu.SemaphoreType.DMA((2, units, count)),
            pltpu.SemaphoreType.DMA((2, units, count)),
            pltpu.SemaphoreType.DMA((4, count)),
            pltpu.SemaphoreType.DMA((4, count)),
            pltpu.SemaphoreType.DMA((2,)),
        ],
        compiler_params=pltpu.CompilerParams(
            collective_id=0, has_side_effects=True, vmem_limit_bytes=50 * 1024 * 1024
        ),
        cost_estimate=pl.CostEstimate(flops=2 * 10**9, bytes_accessed=8 * rows * width * 2, transcendentals=0),
    )(
        query, keyed, values, cotangent, keep, ends, positions, filter_weight,
        skip_gain[None, :], first_factor, second_factor.astype(F32), coefs,
    )


def solution(mesh):
    field = P(("groups", "seq"), "chan")
    return jax.shard_map(
        on_device,
        mesh=mesh,
        in_specs=(
            field, field, field, field, P(("groups", "seq")), P(("groups", "seq"), None),
            P("seq", "chan"), P("chan"), P(), P(), P(None, "seq", None), P(None, "seq", None),
        ),
        out_specs=(field,) * 5,
        check_vma=False,
    )
```

profile of v0, /device:TPU:0, one launch (start us, length us, event | category | flops | bytes accessed | tf_op | source)
XLA Modules:
  0.0 121.1 jit_solution(10759263403761203861)
XLA Ops:
  0.6 0.0 copy-start.7
  0.6 0.0 copy-start.4
  0.7 1.3 %fusion.4 = (s32[1]{0:T(128)}, s32[1]{0:T(128)}) fusion(s32[2048]{0:T(1024)} %param.16), kind=kLoop, calls=%fused_computation.8 | loop fusion | bytes 16 | tf_op jit(solution)/shard_map/slice | solution.py:267
  2.0 1.4 %pad_add_fusion = s32[2]{0:T(128)S(1)} fusion(s32[1]{0:T(128)} %get-tuple-element.5, s32[1]{0:T(128)} %get-tuple-element.6), kind=kLoop, calls=%fused_computation.7 | loop fusion | flops 2 | bytes 16 | tf_op jit(solution)/shard_map/stack | solution.py:267
  3.4 0.0 copy-done.7
  3.4 0.0 copy-done.4
  3.4 0.7 fusion.3
  4.1 0.0 copy-start.5
  4.1 0.0 copy-start.6
  4.1 0.1 broadcast_in_dim.4.ends
  4.2 0.6 copy-done.5
  4.8 0.0 copy-done.6
  4.8 0.0 copy-start
  4.9 0.0 copy-start.1
  4.9 0.0 copy-start.2
  4.9 1.3 %copy.17.pos = bf16[2048,64]{1,0:T(8,128)(2,1)S(1)} copy(bf16[2048,64]{0,1:T(8,128)(2,1)} %param.17) | data formatting | bytes 524288 | tf_op args[5]
  6.2 0.0 copy-done
  6.2 0.0 copy-done.1
  6.2 0.0 copy-done.2
  6.2 109.8 %shard_map.155 = (bf16[2048,256]{1,0:T(8,128)(2,1)S(1)}, bf16[2048,256]{1,0:T(8,128)(2,1)S(1)}, bf16[2048,256]{1,0:T(8,128)(2,1)S(1)}, bf16[2048,256]{1,0:T(8,128)(2,1)}, f32[16,256]{1,0:T(8,128)S(1)}) custom-call(bf16[2048,256]{1,0:T(8,128)(2,1)} %query.1, bf16[2048,256]{1,0:T(8,128)(2,1)} %keyed.1, bf16[2048,256]{1,0:T(8,128)(2,1)} %values.1, ...), custom_call_target="tpu_custom_call" | custom-call | flops 2000000000 | bytes 8388608 | tf_op jit(solution)/shard_map/pallas_call | solution.py:275
  116.0 1.0 copy.23
  117.0 1.0 copy.24
  118.0 0.0 copy-start.3
  118.0 1.0 copy.25
  118.9 0.6 copy-done.3
  119.6 1.0 copy.26
  120.5 0.6 copy.27
  (4 shorter events, 0.0 us)
Async XLA Ops:
  0.6 2.7 %copy-start.7 = (bf16[8,8]{1,0:T(8,128)(2,1)S(1)}, bf16[8,8]{1,0:T(8,128)(2,1)}, u32[]{:S(2)}) copy-start(bf16[8,8]{1,0:T(8,128)(2,1)} %param.21) | copy-start | bytes 388
  0.6 2.7 %copy-start.4 = (s32[2048]{0:T(1024)S(1)}, s32[2048]{0:T(1024)}, u32[]{:S(2)}) copy-start(s32[2048]{0:T(1024)} %param.16) | copy-start | bytes 24580
  4.1 0.7 copy-start.5
  4.1 0.7 copy-start.6
  4.8 1.3 %copy-start = (bf16[256,256]{1,0:T(8,128)(2,1)S(1)}, bf16[256,256]{1,0:T(8,128)(2,1)}, u32[]{:S(2)}) copy-start(bf16[256,256]{1,0:T(8,128)(2,1)} %first.1) | copy-start | bytes 393220
  4.9 1.3 %copy-start.1 = (bf16[16,256]{1,0:T(8,128)(2,1)S(1)}, bf16[16,256]{1,0:T(8,128)(2,1)}, u32[]{:S(2)}) copy-start(bf16[16,256]{1,0:T(8,128)(2,1)} %weight.1) | copy-start | bytes 24580
  4.9 1.3 %copy-start.2 = (f32[256]{0:T(256)S(1)}, f32[256]{0:T(256)}, u32[]{:S(2)}) copy-start(f32[256]{0:T(256)} %param.19) | copy-start | bytes 3076
  118.0 1.6 %copy-start.3 = (bf16[2048,256]{1,0:T(8,128)(2,1)S(1)}, bf16[2048,256]{1,0:T(8,128)(2,1)}, u32[]{:S(2)}) copy-start(bf16[2048,256]{1,0:T(8,128)(2,1)} %get-tuple-element.15) | copy-start | bytes 3145732
where the time goes:
time: 121 us
  Pallas kernels  110 us (91%)
  local copies, waits for them, and re-layouts  8.48 us (7%)
  other arithmetic  2.12 us (2%)
    pallas_call x1, Pallas kernels, on_device(): pl.pallas_call(functools.partial(kernel, count, sections, scale), out_sha...  110 us
    unnamed x22, local copies, waits for them, and re-layouts  7.07 us

commit v1 on v0

v1 whole, which is shorter than its diff:
```python
import functools
import math

import jax
import jax.numpy as jnp
from jax import lax
from jax.experimental import pallas as pl
from jax.experimental.pallas import tpu as pltpu
from jax.sharding import PartitionSpec as P

BLK = 256
LANES = 128
F32 = jnp.float32
BF16 = jnp.bfloat16


def kernel(
    count, sections, scale,
    query_in, keyed_in, values_in, cotangent_in, ids, pos, weight, first, second, self_coef, cross_coef,
    conv, back, keep_out, part_recv,
    query, keyed, values, cotangent, first_t, keep_t, u_all, gt_all, half, fwd_send, fwd_recv, back_send, back_recv,
    pos_send, pos_recv, weight_send, weight_recv, ends_recv, coef_recv, coef_t,
    coef_send, weight_all, filt, dw_keep, dfilt, part_send,
    field_send_sem, field_recv_sem, small_send_sem, small_recv_sem, ends_sem, load_sem,
):
    rows, width = query.shape
    groups = rows // BLK
    quarter = rows // count
    share = weight.shape[0]
    chunks = width // LANES
    me = lax.axis_index("seq")
    others = [(k, lax.rem(me + k, count)) for k in range(1, count)]
    sources = [(k, lax.rem(me + count - k, count)) for k in range(1, count)]

    barrier = pltpu.get_barrier_semaphore()
    for _, other in others:
        pl.semaphore_signal(barrier, inc=1, device_id={"seq": other}, device_id_type=pl.DeviceIdType.MESH)

    def remote(src, dst, send, recv, other):
        return pltpu.make_async_remote_copy(
            src_ref=src, dst_ref=dst, send_sem=send, recv_sem=recv,
            device_id={"seq": other}, device_id_type=pl.DeviceIdType.MESH,
        )

    loads = []
    for chunk in range(chunks):
        cut = pl.ds(chunk * LANES, LANES)
        for n, (far, near) in enumerate(((query_in, query), (cotangent_in, cotangent), (keyed_in, keyed), (values_in, values))):
            loads.append(pltpu.make_async_copy(far.at[:, cut], near.at[:, cut], load_sem.at[chunk, n]))
    order = [4 * chunk + n for n0 in (0, 2) for chunk in range(chunks) for n in (n0, n0 + 1)]
    for at in order:
        loads[at].start()

    coef_send[...] = jnp.zeros_like(coef_send)
    for p in range(count):
        cut = slice(p * quarter, (p + 1) * quarter)
        pos_send[p] = pos[:, cut]
        coef_send[p, :sections, :] = self_coef[:, cut].astype(F32)
        coef_send[p, sections:2 * sections, :] = cross_coef[:, cut].astype(F32)
    weight_send[...] = weight[...].astype(F32)
    first_t[...] = first[...].astype(F32).T.astype(BF16)

    pl.semaphore_wait(barrier, count - 1)

    def small(kind, k, other):
        send, recv = small_send_sem.at[kind, k], small_recv_sem.at[kind, k]
        if kind == 0:
            return remote(pos_send.at[other], pos_recv.at[me], send, recv, other)
        if kind == 1:
            return remote(weight_send, weight_recv.at[me], send, recv, other)
        if kind == 2:
            return remote(coef_send.at[other], coef_recv.at[me], send, recv, other)
        return remote(part_send.at[other], part_recv.at[me], send, recv, other)

    ring = remote(ids, ends_recv, ends_sem.at[0], ends_sem.at[1], lax.rem(me + 1, count))
    ring.start()
    for kind in (2, 1, 0):
        for k, other in others:
            small(kind, k, other).start()
    pos_recv[me] = pos_send[me]
    weight_recv[me] = weight_send[...]
    coef_recv[me] = coef_send[me]

    def forward_copy(unit, k, other):
        return remote(
            fwd_send.at[unit, other], fwd_recv.at[unit, me],
            field_send_sem.at[0, unit, k], field_recv_sem.at[0, unit, k], other,
        )

    def back_copy(unit, k, other):
        return remote(
            back_send.at[unit, other], back_recv.at[unit, me],
            field_send_sem.at[1, unit, k], field_recv_sem.at[1, unit, k], other,
        )

    def lanes(chunk):
        return slice(chunk * LANES, (chunk + 1) * LANES)

    step = min(16, quarter)
    mat = [[second[j, i] for i in range(groups)] for j in range(groups)]

    def forward(unit, chunk, source):
        for j in range(groups):
            x = source[j * BLK:(j + 1) * BLK, lanes(chunk)]
            half[j] = jnp.dot(first_t[...], x, preferred_element_type=F32).astype(BF16)

        if quarter % BLK == 0:
            per = quarter // BLK
            for k, other in others + [(0, me)]:
                mats = [[second[j, other * per + i] for i in range(per)] for j in range(groups)]

                @pl.loop(0, BLK // step)
                def _(r, mats=mats, k=k, other=other):
                    at = pl.multiple_of(r * step, step)
                    xs = [half[j, pl.ds(at, step), :].astype(F32) for j in range(groups)]
                    for i in range(per):
                        y = mats[0][i] * xs[0]
                        for j in range(1, groups):
                            y = y + mats[j][i] * xs[j]
                        place = pl.ds(pl.multiple_of(i * BLK + at, step), step)
                        if k == 0:
                            fwd_recv[unit, me, place, :] = y.astype(BF16)
                        else:
                            fwd_send[unit, other, place, :] = y.astype(BF16)

                if k:
                    forward_copy(unit, k, other).start()
            return

        @pl.loop(0, BLK // step)
        def _(r):
            at = pl.multiple_of(r * step, step)
            xs = [half[j, pl.ds(at, step), :].astype(F32) for j in range(groups)]
            for i in range(groups):
                y = mat[0][i] * xs[0]
                for j in range(1, groups):
                    y = y + mat[j][i] * xs[j]
                place = i * BLK + at
                fwd_send[unit, place // quarter, pl.ds(pl.multiple_of(lax.rem(place, quarter), step), step), :] = y.astype(BF16)

        for k, other in others:
            forward_copy(unit, k, other).start()
        fwd_recv[unit, me] = fwd_send[unit, me]

    for chunk in range(chunks):
        loads[4 * chunk].wait()
        loads[4 * chunk + 1].wait()
        cut = lanes(chunk)
        for j in range(groups):
            at = slice(j * BLK, (j + 1) * BLK)
            gt_all[at, cut] = (cotangent[at, cut].astype(F32) * query[at, cut].astype(F32)).astype(BF16)
        forward(chunk, chunk, gt_all)

    ring.wait_recv()
    here = ids[...]
    above = jnp.concatenate([ends_recv[groups - 1:, BLK - 1:], here[:groups - 1, BLK - 1:]], axis=0)
    before = jnp.concatenate([above, here[:, :BLK - 1]], axis=1)
    spot = (lax.broadcasted_iota(jnp.int32, ids.shape, 0) == 0) & (lax.broadcasted_iota(jnp.int32, ids.shape, 1) == 0)
    keep = jnp.where((here == before) & ((me > 0) | jnp.logical_not(spot)), 1.0, 0.0)
    keep_out[...] = keep
    keep_t[...] = keep.T
    for chunk in range(chunks):
        loads[4 * chunk + 2].wait()
        loads[4 * chunk + 3].wait()
        cut = lanes(chunk)
        for j in range(groups):
            at = slice(j * BLK, (j + 1) * BLK)
            u_all[at, cut] = (keyed[at, cut].astype(F32) * values[at, cut].astype(F32) * keep_t[:, j:j + 1]).astype(BF16)
        forward(chunks + chunk, chunk, u_all)

    for kind in (2, 1, 0):
        for k, source in sources:
            small(kind, k, source).wait_recv()
    for p in range(count):
        weight_all[p * share:(p + 1) * share, :] = weight_recv[p]
    whole = weight_all[...].astype(BF16)
    for p in range(count):
        filt[p] = lax.dot_general(pos_recv[p], whole, (((0,), (0,)), ((), ())), preferred_element_type=F32)
        coef_t[p] = coef_recv[p].T

    def rounded(x):
        return x.astype(BF16).astype(F32)

    def middle(unit, chunk, gated):
        for k, source in sources:
            forward_copy(unit, k, source).wait_recv()

        @pl.loop(0, quarter // step)
        def _(r):
            at = pl.ds(pl.multiple_of(r * step, step), step)
            xs = [fwd_recv[unit, p, at, :].astype(F32) for p in range(count)]
            cols = [coef_t[p, at, :] for p in range(count)]

            def own(k, p):
                return cols[p][:, k:k + 1]

            def cross(k, p):
                return cols[p][:, sections + k:sections + k + 1]

            for k in range(sections):
                xs = [rounded(own(k, p) * xs[p] + cross(k, p) * xs[p ^ (1 << k)]) for p in range(count)]
            for p in range(count):
                if gated:
                    dw_keep[chunk, p, at, :] = xs[p].astype(BF16)
                else:
                    dfilt[p, at, :] = (dw_keep[chunk, p, at, :].astype(F32) * xs[p]).astype(BF16)
            xs = [rounded(xs[p] * filt[p, at, lanes(chunk)]) for p in range(count)]
            for k in reversed(range(sections)):
                xs = [
                    rounded(own(k, p) * xs[p] + cross(k, p ^ (1 << k)) * xs[p ^ (1 << k)])
                    for p in range(count)
                ]
            for p in range(count):
                back_send[unit, p, at, :] = xs[p].astype(BF16)

        for k, other in others:
            back_copy(unit, k, other).start()
        back_recv[unit, me] = back_send[unit, me]
        if not gated:
            total = jnp.dot(pos_recv[0], dfilt[0], preferred_element_type=F32)
            for p in range(1, count):
                total = total + jnp.dot(pos_recv[p], dfilt[p], preferred_element_type=F32)
            total = total * scale
            for p in range(count):
                part_send[p, :, lanes(chunk)] = total[p * share:(p + 1) * share]

    for chunk in range(chunks):
        middle(chunk, chunk, True)
    for chunk in range(chunks):
        middle(chunks + chunk, chunk, False)
    for k, other in others:
        small(3, k, other).start()
    part_recv[me] = part_send[me]

    def final(unit, chunk, target):
        for k, source in sources:
            back_copy(unit, k, source).wait_recv()

        @pl.loop(0, BLK // step)
        def _(r):
            at = pl.multiple_of(r * step, step)
            xs = []
            for i in range(groups):
                place = i * BLK + at
                xs.append(back_recv[unit, place // quarter, pl.ds(pl.multiple_of(lax.rem(place, quarter), step), step), :].astype(F32))
            for j in range(groups):
                y = mat[j][0] * xs[0]
                for i in range(1, groups):
                    y = y + mat[j][i] * xs[i]
                half[j, pl.ds(at, step), :] = y.astype(BF16)

        for j in range(groups):
            target[j * BLK:(j + 1) * BLK, lanes(chunk)] = jnp.dot(
                first[...], half[j], preferred_element_type=F32
            ).astype(BF16)

    for chunk in range(chunks):
        final(chunk, chunk, back)
    for chunk in range(chunks):
        final(chunks + chunk, chunk, conv)

    for k, source in sources:
        small(3, k, source).wait_recv()
    ring.wait_send()
    for k, other in others:
        for kind in range(4):
            small(kind, k, other).wait_send()
        for unit in range(2 * chunks):
            forward_copy(unit, k, other).wait_send()
            back_copy(unit, k, other).wait_send()


def finish(
    query, keyed, values, cotangent, conv, back, keep, gain, parts,
    mixed, grad_query, grad_keyed, grad_values, grad_filter,
):
    keep_t = keep[...].T
    lane = lax.broadcasted_iota(jnp.int32, keep_t.shape, 1)
    kept = jnp.sum(jnp.where(lane == pl.program_id(0), keep_t, 0.0), axis=1, keepdims=True)
    q, c = query[...].astype(F32), cotangent[...].astype(F32)
    k, v = keyed[...].astype(F32), values[...].astype(F32)
    skip = gain[...]
    u = (k * v * kept).astype(BF16).astype(F32)
    total = conv[...].astype(F32) + skip * u
    mixed[...] = (q * total).astype(BF16)
    grad_query[...] = (c * total).astype(BF16)
    gated = (c * q).astype(BF16).astype(F32)
    du = (back[...].astype(F32) + skip * gated) * kept
    grad_keyed[...] = (du * v).astype(BF16)
    grad_values[...] = (du * k).astype(BF16)

    @pl.when(pl.program_id(0) == 0)
    def _():
        total = parts[0]
        for p in range(1, parts.shape[0]):
            total = total + parts[p]
        grad_filter[...] = total


def on_device(
    query, keyed, values, cotangent, segment_ids, positions, filter_weight, skip_gain,
    first_factor, second_factor, self_coef, cross_coef,
):
    count = lax.axis_size("seq")
    sections = self_coef.shape[0]
    rows, width = query.shape
    groups = rows // BLK
    quarter = rows // count
    feats = positions.shape[1]
    share = filter_weight.shape[0]
    chunks = width // LANES
    units = 2 * chunks
    kinds = -(-2 * sections // 8) * 8
    scale = 1.0 / math.sqrt(rows * count)
    vmem = pl.BlockSpec(memory_space=pltpu.VMEM)
    smem = pl.BlockSpec(memory_space=pltpu.SMEM)
    field = jax.ShapeDtypeStruct((rows, width), BF16)
    conv, back, keep, parts = pl.pallas_call(
        functools.partial(kernel, count, sections, scale),
        out_shape=(
            field, field, jax.ShapeDtypeStruct((groups, BLK), F32),
            jax.ShapeDtypeStruct((count, share, width), F32),
        ),
        in_specs=[pl.BlockSpec(memory_space=pl.ANY)] * 4 + [vmem] * 4 + [smem, vmem, vmem],
        out_specs=(vmem,) * 4,
        scratch_shapes=[
            pltpu.VMEM((rows, width), BF16),
            pltpu.VMEM((rows, width), BF16),
            pltpu.VMEM((rows, width), BF16),
            pltpu.VMEM((rows, width), BF16),
            pltpu.VMEM((BLK, BLK), BF16),
            pltpu.VMEM((BLK, groups), F32),
            pltpu.VMEM((rows, width), BF16),
            pltpu.VMEM((rows, width), BF16),
            pltpu.VMEM((groups, BLK, LANES), BF16),
            pltpu.VMEM((units, count, quarter, LANES), BF16),
            pltpu.VMEM((units, count, quarter, LANES), BF16),
            pltpu.VMEM((units, count, quarter, LANES), BF16),
            pltpu.VMEM((units, count, quarter, LANES), BF16),
            pltpu.VMEM((count, feats, quarter), BF16),
            pltpu.VMEM((count, feats, quarter), BF16),
            pltpu.VMEM((share, width), F32),
            pltpu.VMEM((count, share, width), F32),
            pltpu.VMEM((groups, BLK), jnp.int32),
            pltpu.VMEM((count, kinds, quarter), F32),
            pltpu.VMEM((count, quarter, kinds), F32),
            pltpu.VMEM((count, kinds, quarter), F32),
            pltpu.VMEM((feats, width), F32),
            pltpu.VMEM((count, quarter, width), F32),
            pltpu.VMEM((chunks, count, quarter, LANES), BF16),
            pltpu.VMEM((count, quarter, LANES), BF16),
            pltpu.VMEM((count, share, width), F32),
            pltpu.SemaphoreType.DMA((2, units, count)),
            pltpu.SemaphoreType.DMA((2, units, count)),
            pltpu.SemaphoreType.DMA((4, count)),
            pltpu.SemaphoreType.DMA((4, count)),
            pltpu.SemaphoreType.DMA((2,)),
            pltpu.SemaphoreType.DMA((chunks, 4)),
        ],
        compiler_params=pltpu.CompilerParams(
            collective_id=0, has_side_effects=True, vmem_limit_bytes=50 * 1024 * 1024
        ),
        cost_estimate=pl.CostEstimate(flops=2 * 10**9, bytes_accessed=8 * rows * width * 2, transcendentals=0),
    )(
        query, keyed, values, cotangent, segment_ids.reshape(groups, BLK), positions.T, filter_weight,
        first_factor, second_factor.astype(F32), self_coef[:, 0], cross_coef[:, 0],
    )
    block = pl.BlockSpec((BLK, width), lambda j: (j, 0))

    def full(*shape):
        return pl.BlockSpec(shape, lambda j: (0,) * len(shape))

    return pl.pallas_call(
        finish,
        grid=(groups,),
        out_shape=(field, field, field, field, jax.ShapeDtypeStruct((share, width), F32)),
        in_specs=[block] * 6 + [full(groups, BLK), full(1, width), full(count, share, width)],
        out_specs=(block, block, block, block, full(share, width)),
    )(query, keyed, values, cotangent, conv, back, keep, skip_gain[None, :], parts)


def solution(mesh):
    field = P(("groups", "seq"), "chan")
    return jax.shard_map(
        on_device,
        mesh=mesh,
        in_specs=(
            field, field, field, field, P(("groups", "seq")), P(("groups", "seq"), None),
            P("seq", "chan"), P("chan"), P(), P(), P(None, "seq", None), P(None, "seq", None),
        ),
        out_specs=(field,) * 5,
        check_vma=False,
    )
```

time: 121 us -> 125 us (1.033)
  Pallas kernels: 110 us -> 116 us
  other arithmetic: 2.12 us -> 0.01 us
    pallas_call x0 -> x1, Pallas kernels: none -> 8.58 us  [on_device(): pl.pallas_call(finish, grid=(groups,), out_shape=(field, field, field, fi...]
    pallas_call x1, Pallas kernels: 110 us -> 107 us  [on_device(): pl.pallas_call(functools.partial(kernel, count, sections, scale), out_sha...]
    another operation x1 -> x0, other arithmetic: 1.37 us -> none  [on_device(): jnp.stack([segment_ids[0], segment_ids[-1]])[:, None, None]]
    slice x1 -> x0, local copies, waits for them, and re-layouts: 1.34 us -> none  [on_device(): segment_ids[-1]]
where the time goes in v1:
time: 125 us; the launch traced here: 124 us
  Pallas kernels  116 us (93%)
  local copies, waits for them, and re-layouts  7.65 us (6%)
    pallas_call x1, Pallas kernels, on_device(): pl.pallas_call(functools.partial(kernel, count, sections, scale), out_sha...  107 us
    pallas_call x1, Pallas kernels, on_device(): pl.pallas_call(finish, grid=(groups,), out_shape=(field, field, field, fi...  8.58 us
    unnamed x22, local copies, waits for them, and re-layouts  6.92 us

profile of v1, /device:TPU:0, one launch (start us, length us, event | category | flops | bytes accessed | tf_op | source)
XLA Modules:
  0.0 124.3 jit_solution(8374324018507186725)
XLA Ops:
  0.6 0.0 copy-start.10
  0.6 0.0 copy-start.9
  0.7 0.7 copy-done.10
  1.3 0.0 copy-start.7
  1.3 0.0 copy-start.8
  1.3 0.7 reshape.13.ids
  2.0 0.0 copy-done.9
  2.1 0.0 copy-done.7
  2.1 0.0 copy-done.8
  2.1 0.0 copy-start
  2.1 1.2 copy-done
  3.3 0.0 copy-start.5
  3.3 0.9 copy-done.5
  4.2 0.0 copy-start.6
  4.2 0.9 copy-done.6
  5.1 107.4 %shard_map.155 = (bf16[2048,256]{1,0:T(8,128)(2,1)S(1)}, bf16[2048,256]{1,0:T(8,128)(2,1)S(1)}, f32[8,256]{1,0:T(8,128)S(1)}, f32[4,16,256]{2,1,0:T(8,128)S(1)}) custom-call(bf16[2048,256]{1,0:T(8,128)(2,1)S(1)} %copy-done, bf16[2048,256]{1,0:T(8,128)(2,1)} %keyed.1, bf16[2048,256]{1,0:T(8,128)(2,1)} %values.1, bf16[2048,256]{1,0:T(8,128)(2,1)} %cotangent.1, ...), custom_call_target="tpu_custom_call" | custom-call | flops 2000000000 | bytes 8388608 | tf_op jit(solution)/shard_map/pallas_call | solution.py:318
  112.5 0.0 copy-start.1
  112.5 1.0 copy-done.1
  113.5 0.0 copy-start.2
  113.5 1.0 copy-done.2
  114.5 0.0 copy-start.3
  114.5 0.6 copy-done.3
  115.1 0.0 copy-start.4
  115.1 0.6 copy-done.4
  115.7 8.6 %shard_map.156 = (bf16[2048,256]{1,0:T(8,128)(2,1)}, bf16[2048,256]{1,0:T(8,128)(2,1)}, bf16[2048,256]{1,0:T(8,128)(2,1)}, bf16[2048,256]{1,0:T(8,128)(2,1)}, f32[16,256]{1,0:T(8,128)}) custom-call(bf16[2048,256]{1,0:T(8,128)(2,1)} %query.1, bf16[2048,256]{1,0:T(8,128)(2,1)} %keyed.1, bf16[2048,256]{1,0:T(8,128)(2,1)} %values.1, ...), custom_call_target="tpu_custom_call" | custom-call | tf_op jit(solution)/shard_map/pallas_call | solution.py:373
  (1 shorter events, 0.0 us)
Async XLA Ops:
  0.6 0.7 copy-start.10
  0.6 1.4 %copy-start.9 = (bf16[2,1,2048]{2,0,1:T(2,128)(2,1)S(1)}, bf16[2,1,2048]{2,0,1:T(2,128)(2,1)}, u32[]{:S(2)}) copy-start(bf16[2,1,2048]{2,0,1:T(2,128)(2,1)} %param.23) | copy-start | bytes 24580
  1.3 0.7 copy-start.7
  1.3 0.7 copy-start.8
  2.1 1.2 copy-start
  3.3 0.9 copy-start.5
  4.2 0.9 copy-start.6
  112.5 1.0 copy-start.1
  113.5 1.0 copy-start.2
  114.5 0.6 copy-start.3
  115.1 0.6 copy-start.4

commit v2 on v1

--- a/solution.py
+++ b/solution.py
@@ -16,12 +16,14 @@
 
 def kernel(
     count, sections, scale,
-    query_in, keyed_in, values_in, cotangent_in, ids, pos, weight, first, second, self_coef, cross_coef,
-    conv, back, keep_out, part_recv,
+    query_in, keyed_in, values_in, cotangent_in, ids_in, pos_in, weight_in, gain_in, first_in, second_in,
+    self_in, cross_in,
+    mixed_out, query_out, keyed_out, values_out, grad_filter,
+    mixed, grad_query, grad_keyed, grad_values, ids, pos, weight, gain, first, second, self_coef, cross_coef, mat, part_recv,
     query, keyed, values, cotangent, first_t, keep_t, u_all, gt_all, half, fwd_send, fwd_recv, back_send, back_recv,
     pos_send, pos_recv, weight_send, weight_recv, ends_recv, coef_recv, coef_t,
     coef_send, weight_all, filt, dw_keep, dfilt, part_send,
-    field_send_sem, field_recv_sem, small_send_sem, small_recv_sem, ends_sem, load_sem,
+    field_send_sem, field_recv_sem, small_send_sem, small_recv_sem, ends_sem, load_sem, tiny_sem, share_send_sem, share_recv_sem, store_sem,
 ):
     rows, width = query.shape
     groups = rows // BLK
@@ -31,15 +33,27 @@
     me = lax.axis_index("seq")
     others = [(k, lax.rem(me + k, count)) for k in range(1, count)]
     sources = [(k, lax.rem(me + count - k, count)) for k in range(1, count)]
+    feats = pos_in.shape[0]
+    crew = lax.axis_size("chan")
+    split = crew if (feats // crew) % 16 == 0 else 1
+    part = feats // split
+    spot = lax.axis_index("chan")
+    if split > 1:
+        mine = pl.ds(pl.multiple_of(spot * part, part), part)
+        peers = [(k, lax.rem(spot + k, crew)) for k in range(1, crew)]
+    else:
+        mine, peers = slice(None), []
 
     barrier = pltpu.get_barrier_semaphore()
     for _, other in others:
         pl.semaphore_signal(barrier, inc=1, device_id={"seq": other}, device_id_type=pl.DeviceIdType.MESH)
-
-    def remote(src, dst, send, recv, other):
+    for _, peer in peers:
+        pl.semaphore_signal(barrier, inc=1, device_id={"chan": peer}, device_id_type=pl.DeviceIdType.MESH)
+
+    def remote(src, dst, send, recv, other, axis="seq"):
         return pltpu.make_async_remote_copy(
             src_ref=src, dst_ref=dst, send_sem=send, recv_sem=recv,
-            device_id={"seq": other}, device_id_type=pl.DeviceIdType.MESH,
+            device_id={axis: other}, device_id_type=pl.DeviceIdType.MESH,
         )
 
     loads = []
@@ -48,8 +62,19 @@
         for n, (far, near) in enumerate(((query_in, query), (cotangent_in, cotangent), (keyed_in, keyed), (values_in, values))):
             loads.append(pltpu.make_async_copy(far.at[:, cut], near.at[:, cut], load_sem.at[chunk, n]))
     order = [4 * chunk + n for n0 in (0, 2) for chunk in range(chunks) for n in (n0, n0 + 1)]
+    tiny = [
+        pltpu.make_async_copy(far, near, tiny_sem.at[n])
+        for n, (far, near) in enumerate((
+            (pos_in, pos), (self_in, self_coef), (cross_in, cross_coef), (weight_in, weight), (ids_in, ids),
+            (first_in, first), (second_in, second), (gain_in, gain),
+        ))
+    ]
+    for copy in tiny:
+        copy.start()
     for at in order:
         loads[at].start()
+    for copy in tiny:
+        copy.wait()
 
     coef_send[...] = jnp.zeros_like(coef_send)
     for p in range(count):
@@ -58,14 +83,13 @@
         coef_send[p, :sections, :] = self_coef[:, cut].astype(F32)
         coef_send[p, sections:2 * sections, :] = cross_coef[:, cut].astype(F32)
     weight_send[...] = weight[...].astype(F32)
-    first_t[...] = first[...].astype(F32).T.astype(BF16)
-
-    pl.semaphore_wait(barrier, count - 1)
+
+    pl.semaphore_wait(barrier, count - 1 + len(peers))
 
     def small(kind, k, other):
         send, recv = small_send_sem.at[kind, k], small_recv_sem.at[kind, k]
         if kind == 0:
-            return remote(pos_send.at[other], pos_recv.at[me], send, recv, other)
+            return remote(pos_send.at[other, mine], pos_recv.at[me, mine], send, recv, other)
         if kind == 1:
             return remote(weight_send, weight_recv.at[me], send, recv, other)
         if kind == 2:
@@ -77,9 +101,14 @@
     for kind in (2, 1, 0):
         for k, other in others:
             small(kind, k, other).start()
-    pos_recv[me] = pos_send[me]
+    pos_recv[me, mine] = pos_send[me, mine]
     weight_recv[me] = weight_send[...]
     coef_recv[me] = coef_send[me]
+
+    def share_copy(k, peer):
+        return remote(
+            pos_recv.at[:, mine], pos_recv.at[:, mine], share_send_sem.at[k], share_recv_sem.at[k], peer, "chan",
+        )
 
     def forward_copy(unit, k, other):
         return remote(
@@ -97,7 +126,11 @@
         return slice(chunk * LANES, (chunk + 1) * LANES)
 
     step = min(16, quarter)
-    mat = [[second[j, i] for i in range(groups)] for j in range(groups)]
+    first_t[...] = first[...].astype(F32).T.astype(BF16)
+    table = second[...].astype(F32)
+    for j in range(groups):
+        for i in range(groups):
+            mat[j, i] = jnp.broadcast_to(table[j:j + 1, i:i + 1], mat.shape[2:])
 
     def forward(unit, chunk, source):
         for j in range(groups):
@@ -107,7 +140,7 @@
         if quarter % BLK == 0:
             per = quarter // BLK
             for k, other in others + [(0, me)]:
-                mats = [[second[j, other * per + i] for i in range(per)] for j in range(groups)]
+                mats = [[mat[j, other * per + i] for i in range(per)] for j in range(groups)]
 
                 @pl.loop(0, BLK // step)
                 def _(r, mats=mats, k=k, other=other):
@@ -132,9 +165,9 @@
             at = pl.multiple_of(r * step, step)
             xs = [half[j, pl.ds(at, step), :].astype(F32) for j in range(groups)]
             for i in range(groups):
-                y = mat[0][i] * xs[0]
+                y = mat[0, i] * xs[0]
                 for j in range(1, groups):
-                    y = y + mat[j][i] * xs[j]
+                    y = y + mat[j, i] * xs[j]
                 place = i * BLK + at
                 fwd_send[unit, place // quarter, pl.ds(pl.multiple_of(lax.rem(place, quarter), step), step), :] = y.astype(BF16)
 
@@ -153,12 +186,21 @@
 
     ring.wait_recv()
     here = ids[...]
-    above = jnp.concatenate([ends_recv[groups - 1:, BLK - 1:], here[:groups - 1, BLK - 1:]], axis=0)
-    before = jnp.concatenate([above, here[:, :BLK - 1]], axis=1)
-    spot = (lax.broadcasted_iota(jnp.int32, ids.shape, 0) == 0) & (lax.broadcasted_iota(jnp.int32, ids.shape, 1) == 0)
-    keep = jnp.where((here == before) & ((me > 0) | jnp.logical_not(spot)), 1.0, 0.0)
-    keep_out[...] = keep
+    tall = here.shape[0]
+    above = jnp.concatenate([ends_recv[tall - 1:, LANES - 1:], here[:tall - 1, LANES - 1:]], axis=0)
+    before = jnp.concatenate([above, here[:, :LANES - 1]], axis=1)
+    start = (lax.broadcasted_iota(jnp.int32, here.shape, 0) == 0) & (lax.broadcasted_iota(jnp.int32, here.shape, 1) == 0)
+    keep = jnp.where((here == before) & ((me > 0) | jnp.logical_not(start)), 1.0, 0.0)
+    wide = BLK // LANES
+    keep = jnp.concatenate(
+        [jnp.concatenate([keep[j * wide + n:j * wide + n + 1] for n in range(wide)], axis=1) for j in range(groups)], axis=0,
+    )
     keep_t[...] = keep.T
+    if peers:
+        for k, source in sources:
+            small(0, k, source).wait_recv()
+        for k, peer in peers:
+            share_copy(k, peer).start()
     for chunk in range(chunks):
         loads[4 * chunk + 2].wait()
         loads[4 * chunk + 3].wait()
@@ -168,9 +210,18 @@
             u_all[at, cut] = (keyed[at, cut].astype(F32) * values[at, cut].astype(F32) * keep_t[:, j:j + 1]).astype(BF16)
         forward(chunks + chunk, chunk, u_all)
 
-    for kind in (2, 1, 0):
+    for kind in (2, 1):
         for k, source in sources:
             small(kind, k, source).wait_recv()
+    if peers:
+        for k, peer in peers:
+            rest = pl.ds(pl.multiple_of(lax.rem(spot + crew - k, crew) * part, part), part)
+            remote(
+                pos_recv.at[:, rest], pos_recv.at[:, rest], share_send_sem.at[k], share_recv_sem.at[k], peer, "chan",
+            ).wait_recv()
+    else:
+        for k, source in sources:
+            small(0, k, source).wait_recv()
     for p in range(count):
         weight_all[p * share:(p + 1) * share, :] = weight_recv[p]
     whole = weight_all[...].astype(BF16)
@@ -232,7 +283,7 @@
         small(3, k, other).start()
     part_recv[me] = part_send[me]
 
-    def final(unit, chunk, target):
+    def final(unit, chunk, gated):
         for k, source in sources:
             back_copy(unit, k, source).wait_recv()
 
@@ -244,23 +295,55 @@
                 place = i * BLK + at
                 xs.append(back_recv[unit, place // quarter, pl.ds(pl.multiple_of(lax.rem(place, quarter), step), step), :].astype(F32))
             for j in range(groups):
-                y = mat[j][0] * xs[0]
+                y = mat[j, 0] * xs[0]
                 for i in range(1, groups):
-                    y = y + mat[j][i] * xs[i]
+                    y = y + mat[j, i] * xs[i]
                 half[j, pl.ds(at, step), :] = y.astype(BF16)
 
+        cut = lanes(chunk)
+        skip = gain[0:1, cut]
         for j in range(groups):
-            target[j * BLK:(j + 1) * BLK, lanes(chunk)] = jnp.dot(
-                first[...], half[j], preferred_element_type=F32
-            ).astype(BF16)
-
-    for chunk in range(chunks):
-        final(chunk, chunk, back)
-    for chunk in range(chunks):
-        final(chunks + chunk, chunk, conv)
-
+            at = slice(j * BLK, (j + 1) * BLK)
+            y = rounded(jnp.dot(first[...], half[j], preferred_element_type=F32))
+            if gated:
+                du = (y + skip * gt_all[at, cut].astype(F32)) * keep_t[:, j:j + 1]
+                grad_keyed[at, cut] = (du * values[at, cut].astype(F32)).astype(BF16)
+                grad_values[at, cut] = (du * keyed[at, cut].astype(F32)).astype(BF16)
+            else:
+                total = y + skip * u_all[at, cut].astype(F32)
+                mixed[at, cut] = (query[at, cut].astype(F32) * total).astype(BF16)
+                grad_query[at, cut] = (cotangent[at, cut].astype(F32) * total).astype(BF16)
+
+    stores = []
+
+    def store(unit, chunk, pairs):
+        cut = pl.ds(chunk * LANES, LANES)
+        for n, (near, far) in enumerate(pairs):
+            copy = pltpu.make_async_copy(near.at[:, cut], far.at[:, cut], store_sem.at[unit, n])
+            copy.start()
+            stores.append(copy)
+
+    after = ((grad_keyed, keyed_out), (grad_values, values_out))
+    ahead = ((mixed, mixed_out), (grad_query, query_out))
+    for chunk in range(chunks):
+        final(chunk, chunk, True)
+        store(chunk, chunk, after)
+    for chunk in range(chunks - 1):
+        final(chunks + chunk, chunk, False)
+        store(chunks + chunk, chunk, ahead)
     for k, source in sources:
         small(3, k, source).wait_recv()
+    total = part_recv[0]
+    for p in range(1, count):
+        total = total + part_recv[p]
+    grad_filter[...] = total
+    final(2 * chunks - 1, chunks - 1, False)
+    store(2 * chunks - 1, chunks - 1, ahead)
+    for copy in stores:
+        copy.wait()
+
+    for k, peer in peers:
+        share_copy(k, peer).wait_send()
     ring.wait_send()
     for k, other in others:
         for kind in range(4):
@@ -268,33 +351,6 @@
         for unit in range(2 * chunks):
             forward_copy(unit, k, other).wait_send()
             back_copy(unit, k, other).wait_send()
-
-
-def finish(
-    query, keyed, values, cotangent, conv, back, keep, gain, parts,
-    mixed, grad_query, grad_keyed, grad_values, grad_filter,
-):
-    keep_t = keep[...].T
-    lane = lax.broadcasted_iota(jnp.int32, keep_t.shape, 1)
-    kept = jnp.sum(jnp.where(lane == pl.program_id(0), keep_t, 0.0), axis=1, keepdims=True)
-    q, c = query[...].astype(F32), cotangent[...].astype(F32)
-    k, v = keyed[...].astype(F32), values[...].astype(F32)
-    skip = gain[...]
-    u = (k * v * kept).astype(BF16).astype(F32)
-    total = conv[...].astype(F32) + skip * u
-    mixed[...] = (q * total).astype(BF16)
-    grad_query[...] = (c * total).astype(BF16)
-    gated = (c * q).astype(BF16).astype(F32)
-    du = (back[...].astype(F32) + skip * gated) * kept
-    grad_keyed[...] = (du * v).astype(BF16)
-    grad_values[...] = (du * k).astype(BF16)
-
-    @pl.when(pl.program_id(0) == 0)
-    def _():
-        total = parts[0]
-        for p in range(1, parts.shape[0]):
-            total = total + parts[p]
-        grad_filter[...] = total
 
 
 def on_device(
@@ -313,17 +369,29 @@
     kinds = -(-2 * sections // 8) * 8
     scale = 1.0 / math.sqrt(rows * count)
     vmem = pl.BlockSpec(memory_space=pltpu.VMEM)
-    smem = pl.BlockSpec(memory_space=pltpu.SMEM)
     field = jax.ShapeDtypeStruct((rows, width), BF16)
-    conv, back, keep, parts = pl.pallas_call(
+    crew = lax.axis_size("chan")
+    tall = rows // LANES
+    return pl.pallas_call(
         functools.partial(kernel, count, sections, scale),
-        out_shape=(
-            field, field, jax.ShapeDtypeStruct((groups, BLK), F32),
-            jax.ShapeDtypeStruct((count, share, width), F32),
-        ),
-        in_specs=[pl.BlockSpec(memory_space=pl.ANY)] * 4 + [vmem] * 4 + [smem, vmem, vmem],
-        out_specs=(vmem,) * 4,
+        out_shape=(field, field, field, field, jax.ShapeDtypeStruct((share, width), F32)),
+        in_specs=[pl.BlockSpec(memory_space=pltpu.HBM)] * 12,
+        out_specs=(pl.BlockSpec(memory_space=pltpu.HBM),) * 4 + (vmem,),
         scratch_shapes=[
+            pltpu.VMEM((rows, width), BF16),
+            pltpu.VMEM((rows, width), BF16),
+            pltpu.VMEM((rows, width), BF16),
+            pltpu.VMEM((rows, width), BF16),
+            pltpu.VMEM((tall, LANES), jnp.int32),
+            pltpu.VMEM((feats, rows), BF16),
+            pltpu.VMEM((share, width), BF16),
+            pltpu.VMEM((1, width), F32),
+            pltpu.VMEM((BLK, BLK), BF16),
+            pltpu.VMEM(second_factor.shape, BF16),
+            pltpu.VMEM((sections, rows), BF16),
+            pltpu.VMEM((sections, rows), BF16),
+            pltpu.VMEM((groups, groups, min(16, quarter), LANES), F32),
+            pltpu.VMEM((count, share, width), F32),
             pltpu.VMEM((rows, width), BF16),
             pltpu.VMEM((rows, width), BF16),
             pltpu.VMEM((rows, width), BF16),
@@ -341,7 +409,7 @@
             pltpu.VMEM((count, feats, quarter), BF16),
             pltpu.VMEM((share, width), F32),
             pltpu.VMEM((count, share, width), F32),
-            pltpu.VMEM((groups, BLK), jnp.int32),
+            pltpu.VMEM((tall, LANES), jnp.int32),
             pltpu.VMEM((count, kinds, quarter), F32),
             pltpu.VMEM((count, quarter, kinds), F32),
             pltpu.VMEM((count, kinds, quarter), F32),
@@ -356,27 +424,19 @@
             pltpu.SemaphoreType.DMA((4, count)),
             pltpu.SemaphoreType.DMA((2,)),
             pltpu.SemaphoreType.DMA((chunks, 4)),
+            pltpu.SemaphoreType.DMA((8,)),
+            pltpu.SemaphoreType.DMA((crew,)),
+            pltpu.SemaphoreType.DMA((crew,)),
+            pltpu.SemaphoreType.DMA((units, 2)),
         ],
         compiler_params=pltpu.CompilerParams(
-            collective_id=0, has_side_effects=True, vmem_limit_bytes=50 * 1024 * 1024
+            collective_id=0, has_side_effects=True, vmem_limit_bytes=58 * 1024 * 1024
         ),
         cost_estimate=pl.CostEstimate(flops=2 * 10**9, bytes_accessed=8 * rows * width * 2, transcendentals=0),
     )(
-        query, keyed, values, cotangent, segment_ids.reshape(groups, BLK), positions.T, filter_weight,
-        first_factor, second_factor.astype(F32), self_coef[:, 0], cross_coef[:, 0],
+        query, keyed, values, cotangent, segment_ids.reshape(tall, LANES), positions.T, filter_weight,
+        skip_gain[None, :], first_factor, second_factor, self_coef[:, 0], cross_coef[:, 0],
     )
-    block = pl.BlockSpec((BLK, width), lambda j: (j, 0))
-
-    def full(*shape):
-        return pl.BlockSpec(shape, lambda j: (0,) * len(shape))
-
-    return pl.pallas_call(
-        finish,
-        grid=(groups,),
-        out_shape=(field, field, field, field, jax.ShapeDtypeStruct((share, width), F32)),
-        in_specs=[block] * 6 + [full(groups, BLK), full(1, width), full(count, share, width)],
-        out_specs=(block, block, block, block, full(share, width)),
-    )(query, keyed, values, cotangent, conv, back, keep, skip_gain[None, :], parts)
 
 
 def solution(mesh):

time: 125 us -> 115 us (0.920)
  Pallas kernels: 116 us -> 107 us
    pallas_call x1 -> x0, Pallas kernels: 8.58 us -> none  [on_device(): pl.pallas_call(finish, grid=(groups,), out_shape=(field, field, field, fi...]
    unnamed x22 -> x13, local copies, waits for them, and re-layouts: 6.92 us -> 7.14 us
where the time goes in v2:
time: 115 us
  Pallas kernels  107 us (93%)
  local copies, waits for them, and re-layouts  7.14 us (6%)
    pallas_call x1, Pallas kernels, on_device(): pl.pallas_call(functools.partial(kernel, count, sections, scale), out_sha...  107 us
    unnamed x13, local copies, waits for them, and re-layouts  7.14 us

profile of v2, /device:TPU:0, one launch (start us, length us, event | category | flops | bytes accessed | tf_op | source)
XLA Modules:
  0.0 114.6 jit_solution(9254854477561658029)
XLA Ops:
  0.6 106.8 %shard_map.155 = (bf16[2048,256]{1,0:T(8,128)(2,1)}, bf16[2048,256]{1,0:T(8,128)(2,1)}, bf16[2048,256]{1,0:T(8,128)(2,1)}, bf16[2048,256]{1,0:T(8,128)(2,1)}, f32[16,256]{1,0:T(8,128)}) custom-call(bf16[2048,256]{1,0:T(8,128)(2,1)} %query_in.1, bf16[2048,256]{1,0:T(8,128)(2,1)} %keyed_in.1, bf16[2048,256]{1,0:T(8,128)(2,1)} %values_in.1, ...), custom_call_target="tpu_custom_call" | custom-call | flops 2000000000 | bytes 8388608 | tf_op jit(solution)/shard_map/pallas_call | solution.py:375
  107.5 0.0 copy-start.2
  107.5 2.4 %copy.22 = bf16[2048,256]{1,0:T(8,128)(2,1)} copy(bf16[2048,256]{1,0:T(8,128)(2,1)} %get-tuple-element.10) | data formatting | bytes 2097152
  109.8 0.0 copy-done.2
  109.8 0.0 copy-start.1
  109.8 1.0 copy.23
  110.8 0.6 copy-done.1
  111.4 0.0 copy-start
  111.4 1.0 copy.24
  112.4 0.6 copy-done
  113.0 0.0 copy-start.3
  113.0 1.0 copy.25
  114.0 0.0 copy-done.3
  114.0 0.6 copy.26
Async XLA Ops:
  107.5 2.4 %copy-start.2 = (bf16[2048,256]{1,0:T(8,128)(2,1)S(1)}, bf16[2048,256]{1,0:T(8,128)(2,1)}, u32[]{:S(2)}) copy-start(bf16[2048,256]{1,0:T(8,128)(2,1)} %get-tuple-element.11) | copy-start | bytes 3145732
  109.8 1.6 %copy-start.1 = (bf16[2048,256]{1,0:T(8,128)(2,1)S(1)}, bf16[2048,256]{1,0:T(8,128)(2,1)}, u32[]{:S(2)}) copy-start(bf16[2048,256]{1,0:T(8,128)(2,1)} %get-tuple-element.12) | copy-start | bytes 3145732
  111.4 1.6 %copy-start = (bf16[2048,256]{1,0:T(8,128)(2,1)S(1)}, bf16[2048,256]{1,0:T(8,128)(2,1)}, u32[]{:S(2)}) copy-start(bf16[2048,256]{1,0:T(8,128)(2,1)} %get-tuple-element.13) | copy-start | bytes 3145732
  113.0 1.0 copy-start.3

commit v3 on v2

--- a/solution.py
+++ b/solution.py
@@ -430,7 +430,7 @@
             pltpu.SemaphoreType.DMA((units, 2)),
         ],
         compiler_params=pltpu.CompilerParams(
-            collective_id=0, has_side_effects=True, vmem_limit_bytes=58 * 1024 * 1024
+            collective_id=0, has_side_effects=True, vmem_limit_bytes=49 * 1024 * 1024
         ),
         cost_estimate=pl.CostEstimate(flops=2 * 10**9, bytes_accessed=8 * rows * width * 2, transcendentals=0),
     )(

time: 115 us -> 116 us (level)
  local copies, waits for them, and re-layouts: 7.14 us -> 9.79 us
  Pallas kernels: 107 us -> 105 us
    unnamed x13 -> x21, local copies, waits for them, and re-layouts: 7.14 us -> 9.79 us
    pallas_call x1, Pallas kernels: 107 us -> 105 us  [on_device(): pl.pallas_call(functools.partial(kernel, count, sections, scale), out_sha...]
where the time goes in v3:
time: 116 us
  Pallas kernels  105 us (91%)
  local copies, waits for them, and re-layouts  9.79 us (8%)
    pallas_call x1, Pallas kernels, on_device(): pl.pallas_call(functools.partial(kernel, count, sections, scale), out_sha...  105 us
    unnamed x21, local copies, waits for them, and re-layouts  9.79 us

profile of v3, /device:TPU:0, one launch (start us, length us, event | category | flops | bytes accessed | tf_op | source)
XLA Modules:
  0.0 115.6 jit_solution(8749450438082599237)
XLA Ops:
  0.6 0.0 copy-start.2
  0.6 0.0 copy-start.7
  0.7 0.7 copy-done.2
  1.3 0.0 copy-done.7
  1.3 0.0 copy-start
  1.3 0.9 copy-done
  2.3 0.0 copy-start.1
  2.3 0.9 copy-done.1
  3.2 0.0 copy-start.3
  3.2 0.7 copy-done.3
  3.9 0.0 copy-start.4
  3.9 0.7 copy-done.4
  4.6 0.0 copy-start.5
  4.6 0.7 copy-done.5
  5.3 0.0 copy-start.6
  5.3 0.7 copy-done.6
  6.0 105.2 %shard_map.155 = (bf16[2048,256]{1,0:T(8,128)(2,1)S(1)}, bf16[2048,256]{1,0:T(8,128)(2,1)S(1)}, bf16[2048,256]{1,0:T(8,128)(2,1)S(1)}, bf16[2048,256]{1,0:T(8,128)(2,1)S(1)}, f32[16,256]{1,0:T(8,128)S(1)}) custom-call(bf16[2048,256]{1,0:T(8,128)(2,1)} %query_in.1, bf16[2048,256]{1,0:T(8,128)(2,1)} %keyed_in.1, bf16[2048,256]{1,0:T(8,128)(2,1)} %values_in.1, ...), custom_call_target="tpu_custom_call" | custom-call | flops 2000000000 | bytes 8388608 | tf_op jit(solution)/shard_map/pallas_call | solution.py:375
  111.2 1.0 copy.22
  112.1 1.0 copy.23
  113.1 1.0 copy.24
  114.1 1.0 copy.25
  115.0 0.6 copy.26
Async XLA Ops:
  0.6 0.7 copy-start.2
  0.6 0.7 copy-start.7
  1.3 1.0 copy-start
  2.3 0.9 copy-start.1
  3.2 0.7 copy-start.3
  3.9 0.7 copy-start.4
  4.6 0.7 copy-start.5
  5.3 0.7 copy-start.6
